TPU v7x, 32 devices: a whole 2x2x4 slice. The times are simulated.
32 devices in a mesh: gx: 8 (over y, x, core), gy: 4 (over z).
Axes of the slice: x: 2, y: 2, z: 4, core: 2. Of those that a mesh axis runs over, the one named last changes fastest.
Arguments:
- water_state: float32 [3, 512, 2048], P(None, 'gy', 'gx'), may hold values from -0.5 to 1.5, as said below
- bed_level: float32 [512, 2048], P('gy', 'gx'), may hold values from -0.1 to 0.1
- active_tiles: int32 [1, 4, 16], replicated, may hold values from 0 to 1, as said below
- roughness: int32 [4, 16], replicated, may hold values from 0 to 3
Outputs:
- water_out: float32 [3, 512, 2048], P(None, 'gy', 'gx')
Inputs may be any that keep to these rules, and one draw needn't show every extreme that they name: `water_state`: entry 0 along the first dimension is the water depth, at least 0.5 everywhere; entries 1 and 2 are the discharges along the columns and along the rows, of magnitude at most 0.5. `active_tiles`: whole blocks of 2 tiles side by side along the columns, starting at multiples of 2, may be off the list together.
All inputs are finite; a program needn't handle non-finite values.
Results may differ from a plain program's by a relative error of at most 0.0003.
Values sent between devices are 32-bit elements; how exact they have to be, the bound alone decides.
A program may use at most 64 MiB of HBM per device.

v0:
```python
from functools import partial

import jax
import jax.numpy as jnp
from jax import lax
from jax.sharding import PartitionSpec as P

GRAVITY = 9.81
SPACING = 2.0
TIME_STEP = 0.1
MANNING = (0.03, 0.06, 0.1, 0.15)
ROW_SIGNS = (1.0, 1.0, -1.0)
COL_SIGNS = (1.0, -1.0, 1.0)


def with_halo(x, sides, width):
    for axis, dim in sides:
        devices, length = (lax.axis_size(axis), x.shape[dim])
        up = [(i, (i + 1) % devices) for i in range(devices - 1)]
        down = [(j, i) for i, j in up]
        last = lax.slice_in_dim(x, length - width, length, axis=dim)
        initial = lax.slice_in_dim(x, 0, width, axis=dim)
        before = lax.ppermute(last, axis, up)
        after = lax.ppermute(initial, axis, down)
        x = jnp.concatenate([before, x, after], axis=dim)
    return x


def minmod_limit(lower, upper):
    return jnp.where(
        lower * upper > 0.0, jnp.sign(lower) * jnp.minimum(jnp.abs(lower), jnp.abs(upper)), 0.0
    )


def cut_along(array, begin, finish, axis):
    return lax.slice_in_dim(array, begin, finish, axis=axis)


def face_states(field, axis, interior):
    between = cut_along(field, 1, interior + 4, axis) - cut_along(field, 0, interior + 3, axis)
    slopes = minmod_limit(
        cut_along(between, 0, interior + 2, axis), cut_along(between, 1, interior + 3, axis)
    )
    left_side = cut_along(field, 1, interior + 2, axis) + 0.5 * cut_along(
        slopes, 0, interior + 1, axis
    )
    right_side = cut_along(field, 2, interior + 3, axis) - 0.5 * cut_along(
        slopes, 1, interior + 2, axis
    )
    return (left_side, right_side)


def physical_flux(water_depth, normal_flow, tangent_flow):
    velocity = normal_flow / water_depth
    fluxes = (
        normal_flow,
        normal_flow * velocity + 0.5 * GRAVITY * water_depth * water_depth,
        tangent_flow * velocity,
    )
    return (fluxes, jnp.abs(velocity) + jnp.sqrt(GRAVITY * water_depth))


def rusanov_flux(left_side, right_side):
    left_flux, left_speed = physical_flux(*left_side)
    right_flux, right_speed = physical_flux(*right_side)
    fastest = jnp.maximum(left_speed, right_speed)
    return tuple(
        (
            0.5 * (a + b) - 0.5 * fastest * (r - l)
            for a, b, l, r in zip(left_flux, right_flux, left_side, right_side)
        )
    )


def tendency(extended, bed_part, friction, active, row_count, col_count):
    water_depth, flow_x, flow_y = (extended[0], extended[1], extended[2])
    across = [
        face_states(f[2 : row_count + 2, :], 1, col_count) for f in (water_depth, flow_x, flow_y)
    ]
    flux_x = rusanov_flux(tuple((p[0] for p in across)), tuple((p[1] for p in across)))
    downward = [
        face_states(f[:, 2 : col_count + 2], 0, row_count) for f in (water_depth, flow_y, flow_x)
    ]
    flux_y = rusanov_flux(tuple((p[0] for p in downward)), tuple((p[1] for p in downward)))
    centre_depth = water_depth[2 : row_count + 2, 2 : col_count + 2]
    centre_x = flow_x[2 : row_count + 2, 2 : col_count + 2]
    centre_y = flow_y[2 : row_count + 2, 2 : col_count + 2]
    slope_x = (
        bed_part[2 : row_count + 2, 3 : col_count + 3]
        - bed_part[2 : row_count + 2, 1 : col_count + 1]
    ) / (2.0 * SPACING)
    slope_y = (
        bed_part[3 : row_count + 3, 2 : col_count + 2]
        - bed_part[1 : row_count + 1, 2 : col_count + 2]
    ) / (2.0 * SPACING)
    resistance = (
        GRAVITY
        * friction
        * jnp.sqrt(centre_x * centre_x + centre_y * centre_y)
        / (centre_depth * jnp.exp(jnp.log(centre_depth) * (4.0 / 3.0)))
    )

    def along_x(f):
        return (f[:, 1:] - f[:, :-1]) / SPACING

    def along_y(f):
        return (f[1:, :] - f[:-1, :]) / SPACING

    change_depth = -(along_x(flux_x[0]) + along_y(flux_y[0]))
    change_x = (
        -(along_x(flux_x[1]) + along_y(flux_y[2]))
        - GRAVITY * centre_depth * slope_x
        - resistance * centre_x
    )
    change_y = (
        -(along_x(flux_x[2]) + along_y(flux_y[1]))
        - GRAVITY * centre_depth * slope_y
        - resistance * centre_y
    )
    return jnp.stack([change_depth, change_x, change_y]) * active


def friction_table(roughness):
    table = jnp.zeros(roughness.shape, jnp.float32)
    for level, value in enumerate(MANNING):
        table = table + jnp.where(roughness == level, value * value, 0.0)
    return table


def mirror_edges(extended, rim_width, row_sign, col_sign, borders):
    at_top, at_bottom, at_left, at_right = borders
    upper_rim = jnp.flip(extended[..., rim_width : 2 * rim_width, :], axis=-2) * row_sign
    lower_rim = jnp.flip(extended[..., -2 * rim_width : -rim_width, :], axis=-2) * row_sign
    extended = jnp.concatenate(
        [
            jnp.where(at_top, upper_rim, extended[..., :rim_width, :]),
            extended[..., rim_width:-rim_width, :],
            jnp.where(at_bottom, lower_rim, extended[..., -rim_width:, :]),
        ],
        axis=-2,
    )
    left_rim = jnp.flip(extended[..., rim_width : 2 * rim_width], axis=-1) * col_sign
    right_rim = jnp.flip(extended[..., -2 * rim_width : -rim_width], axis=-1) * col_sign
    return jnp.concatenate(
        [
            jnp.where(at_left, left_rim, extended[..., :rim_width]),
            extended[..., rim_width:-rim_width],
            jnp.where(at_right, right_rim, extended[..., -rim_width:]),
        ],
        axis=-1,
    )


def region_table(padded, row_index, col_index, per_device, tile_size, extension):
    corner_table = lax.dynamic_slice(
        padded, (row_index, col_index * per_device), (3, per_device + 2)
    )
    row_repeats = jnp.array([extension, tile_size, extension], jnp.int32)
    taller = jnp.repeat(
        corner_table, row_repeats, axis=0, total_repeat_length=tile_size + 2 * extension
    )
    col_repeats = jnp.array([extension] + [tile_size] * per_device + [extension], jnp.int32)
    return jnp.repeat(
        taller, col_repeats, axis=1, total_repeat_length=tile_size * per_device + 2 * extension
    )


def working(operands, row_count, span_cols):
    return tendency(operands[0], operands[1], operands[2], operands[3], row_count, span_cols)


def resting(operands, row_count, span_cols):
    return jnp.zeros((3, row_count, span_cols), jnp.float32)


def tile_pieces(extended, bed_part, friction, active, start, width):
    return (
        lax.dynamic_slice_in_dim(extended, start, width + 4, axis=2),
        lax.dynamic_slice_in_dim(bed_part, start, width + 4, axis=1),
        lax.dynamic_slice_in_dim(friction, start, width, axis=1),
        lax.dynamic_slice_in_dim(active, start, width, axis=1),
    )


def run_tile(operands, wanted, width):
    going = jnp.logical_and(wanted, jnp.max(operands[3]) > 0.0)
    return lax.cond(
        going,
        partial(working, row_count=width, span_cols=width),
        partial(resting, row_count=width, span_cols=width),
        operands,
    )


def assemble(results):
    parts = [results[0]] + [piece for piece in results[1:]]
    return jnp.concatenate(parts, axis=-1)


def local_rates(extended, bed_part, friction, active, extension, setup):
    tile_size, per_device, skipping = (setup[0], setup[1], setup[2])
    width = tile_size + 2 * extension
    results = [
        run_tile(
            tile_pieces(extended, bed_part, friction, active, number * tile_size, width),
            jnp.asarray(True),
            width,
        )
        for number in range(per_device)
    ]
    return assemble(results)


def rim_tendency(
    fields, borders, row_signs, col_signs, bed_inner, friction_inner, active_inner, rate_fn, setup
):
    extended = with_halo(fields, (("gx", 2), ("gy", 1)), 2)
    extended = mirror_edges(extended, 2, row_signs, col_signs, borders)
    return rate_fn(extended, bed_inner, friction_inner, active_inner, 0, setup)


def body(water_state, bed_level, active_tiles, roughness):
    tile_size, device_cols = bed_level.shape
    per_device = device_cols // tile_size
    row_index = lax.axis_index("gy")
    col_index = lax.axis_index("gx")
    borders = (
        row_index == 0,
        row_index == lax.axis_size("gy") - 1,
        col_index == 0,
        col_index == lax.axis_size("gx") - 1,
    )
    row_signs = jnp.array(ROW_SIGNS, jnp.float32).reshape(3, 1, 1)
    col_signs = jnp.array(COL_SIGNS, jnp.float32).reshape(3, 1, 1)
    bed_outer = with_halo(bed_level, (("gx", 1), ("gy", 0)), 4)
    bed_outer = mirror_edges(bed_outer, 4, 1.0, 1.0, borders)
    bed_inner = bed_outer[2:-2, 2:-2]
    friction_padded = jnp.pad(friction_table(roughness), 1, mode="edge")
    friction_inner = region_table(friction_padded, row_index, col_index, per_device, tile_size, 0)
    fields = water_state
    flags_padded = jnp.pad(active_tiles[0].astype(jnp.float32), 1, mode="edge")
    active_inner = region_table(flags_padded, row_index, col_index, per_device, tile_size, 0)
    setup = (tile_size, per_device, True, None, None)
    section_one = fields + TIME_STEP * rim_tendency(
        fields,
        borders,
        row_signs,
        col_signs,
        bed_inner,
        friction_inner,
        active_inner,
        local_rates,
        setup,
    )
    fields = 0.5 * fields + 0.5 * (
        section_one
        + TIME_STEP
        * rim_tendency(
            section_one,
            borders,
            row_signs,
            col_signs,
            bed_inner,
            friction_inner,
            active_inner,
            local_rates,
            setup,
        )
    )
    return fields


def solution(mesh):
    return jax.shard_map(
        body,
        mesh=mesh,
        in_specs=(P(None, "gy", "gx"), P("gy", "gx"), P(), P()),
        out_specs=P(None, "gy", "gx"),
        check_vma=False,
    )
```

profile of v0, /device:TPU:12, one launch (start us, length us, event | category | flops | bytes accessed | tf_op | source)
XLA Modules:
  0.0 73.4 jit_solution(4106821262172417580)
XLA Ops:
  0.0 0.9 %fusion.178 = (f32[128,4]{1,0:T(8,128)S(1)}, f32[128,4]{1,0:T(8,128)S(1)}) fusion(f32[128,256]{1,0:T(8,128)} %param.31), kind=kLoop, calls=%fused_computation.446 | loop fusion | bytes 8192 | tf_op jit(solution)/shard_map/slice | solution.py:21
  1.0 1.9 %collective-permute-start.4 = (f32[128,4]{1,0:T(8,128)S(1)}, f32[128,4]{1,0:T(8,128)S(1)}, u32[]{:S(2)}, u32[]{:S(2)}) collective-permute-start(f32[128,4]{1,0:T(8,128)S(1)} %get-tuple-element.233), channel_id=1, source_target_pairs={{0,4},{4,8},{8,12},{12,16},{16,20},{20,24},{24,28},{1,5},{5,9},{9,... | collective-permute-start | bytes 6152 | tf_op jit(solution)/shard_map/ppermute | solution.py:23
  2.9 4.5 %collective-permute-start.5 = (f32[128,4]{1,0:T(8,128)S(1)}, f32[128,4]{1,0:T(8,128)S(1)}, u32[]{:S(2)}, u32[]{:S(2)}) collective-permute-start(f32[128,4]{1,0:T(8,128)S(1)} %get-tuple-element.234), channel_id=1, source_target_pairs={{4,0},{8,4},{12,8},{16,12},{20,16},{24,20},{28,24},{5,1},{9,5},{13... | collective-permute-start | bytes 6152 | tf_op jit(solution)/shard_map/ppermute | solution.py:24
  7.4 1.1 %fusion.175 = (f32[3,128,2]{2,1,0:T(8,128)S(1)}, f32[3,128,2]{2,1,0:T(8,128)S(1)}) fusion(f32[3,128,256]{2,1,0:T(8,128)} %param.30), kind=kLoop, calls=%fused_computation.443 | loop fusion | bytes 12288 | tf_op jit(solution)/shard_map/slice | solution.py:21
  8.6 1.9 %collective-permute-start = (f32[3,128,2]{2,1,0:T(8,128)S(1)}, f32[3,128,2]{2,1,0:T(8,128)S(1)}, u32[]{:S(2)}, u32[]{:S(2)}) collective-permute-start(f32[3,128,2]{2,1,0:T(8,128)S(1)} %get-tuple-element.219), channel_id=1, source_target_pairs={{0,4},{4,8},{8,12},{12,16},{16,20},{20,24},{24,28},{1,5},{5,9},{9,... | collective-permute-start | bytes 9224 | tf_op jit(solution)/shard_map/ppermute | solution.py:23
  10.5 4.5 %collective-permute-start.1 = (f32[3,128,2]{2,1,0:T(8,128)S(1)}, f32[3,128,2]{2,1,0:T(8,128)S(1)}, u32[]{:S(2)}, u32[]{:S(2)}) collective-permute-start(f32[3,128,2]{2,1,0:T(8,128)S(1)} %get-tuple-element.220), channel_id=1, source_target_pairs={{4,0},{8,4},{12,8},{16,12},{20,16},{24,20},{28,24},{5,1},{9,5},{13... | collective-permute-start | bytes 9224 | tf_op jit(solution)/shard_map/ppermute | solution.py:24
  15.1 0.7 copy-done.5
  15.8 0.7 copy-done.6
  16.5 0.6 copy-done.4
  17.5 0.6 gather_fusion
  18.2 0.7 gather_fusion.2
  19.0 0.8 %gather_fusion.3 = f32[256,128]{1,0:T(8,128)S(1)} fusion(f32[128,4]{0,1:T(4,128)S(1)} %copy.12, s32[1024]{0:T(1024)S(1)} %pad_clamp_fusion), kind=kCustom, calls=%fused_computation.3.clone | custom fusion | bytes 263168 | tf_op jit(solution)/shard_map/jit(_take)/gather | solution.py:163
  19.7 0.7 gather_fusion.1
  20.5 0.6 slice_reduce_fusion.1
  22.6 2.4 %collective-permute-start.7 = (f32[4,264]{1,0:T(4,128)S(1)}, f32[4,264]{1,0:T(4,128)S(1)}, u32[]{:S(2)}, u32[]{:S(2)}) collective-permute-start(f32[4,264]{1,0:T(4,128)S(1)} %get-tuple-element.221), channel_id=1, source_target_pairs={{1,0},{2,1},{3,2},{5,4},{6,5},{7,6},{9,8},{10,9},{11,10},{13,12},{... | collective-permute-start | bytes 12680 | tf_op jit(solution)/shard_map/ppermute | solution.py:24
  25.1 3.5 %collective-permute-start.6 = (f32[4,264]{1,0:T(4,128)S(1)}, f32[4,264]{1,0:T(4,128)S(1)}, u32[]{:S(2)}, u32[]{:S(2)}) collective-permute-start(f32[4,264]{1,0:T(4,128)S(1)} %get-tuple-element.222), channel_id=1, source_target_pairs={{0,1},{1,2},{2,3},{4,5},{5,6},{6,7},{8,9},{9,10},{10,11},{12,13},{... | collective-permute-start | bytes 12680 | tf_op jit(solution)/shard_map/ppermute | solution.py:23
  28.8 3.5 %collective-permute-start.2 = (f32[3,2,260]{2,1,0:T(2,128)S(1)}, f32[3,2,260]{2,1,0:T(2,128)S(1)}, u32[]{:S(2)}, u32[]{:S(2)}) collective-permute-start(f32[3,2,260]{2,1,0:T(2,128)S(1)} %get-tuple-element.203), channel_id=1, source_target_pairs={{0,1},{1,2},{2,3},{4,5},{5,6},{6,7},{8,9},{9,10},{10,11},{12,13},{... | collective-permute-start | bytes 18728 | tf_op jit(solution)/shard_map/ppermute | solution.py:23
  32.4 2.4 %collective-permute-start.3 = (f32[3,2,260]{2,1,0:T(2,128)S(1)}, f32[3,2,260]{2,1,0:T(2,128)S(1)}, u32[]{:S(2)}, u32[]{:S(2)}) collective-permute-start(f32[3,2,260]{2,1,0:T(2,128)S(1)} %get-tuple-element.204), channel_id=1, source_target_pairs={{1,0},{2,1},{3,2},{5,4},{6,5},{7,6},{9,8},{10,9},{11,10},{13,12},{... | collective-permute-start | bytes 18728 | tf_op jit(solution)/shard_map/ppermute | solution.py:24
  35.2 0.2 rev.45
  35.4 0.2 rev.47
  35.8 0.2 pad_maximum_fusion.8
  36.0 2.0 %collective-permute-done.3 = f32[3,2,260]{2,1,0:T(2,128)S(1)} collective-permute-done((f32[3,2,260]{2,1,0:T(2,128)S(1)}, f32[3,2,260]{2,1,0:T(2,128)S(1)}, u32[]{:S(2)}, u32[]{:S(2)}) %collective-permute-start.3) | collective-permute-done | bytes 6272 | tf_op jit(solution)/shard_map/ppermute | solution.py:24
  38.1 0.3 pad_maximum_fusion
  38.7 0.6 rev.42
  39.3 0.6 rev.46
  40.1 0.2 pad_maximum_fusion.1
  40.4 2.9 %conditional.4 = (f32[3,128,128]{2,1,0:T(8,128)S(1)}) conditional(s32[]{:T(128)} %convert_element_type.16, () %tuple.47, (f32[3,132,258]{2,1,0:T(8,128)S(1)}, f32[132,132]{1,0:T(8,128)S(1)}, f32[128,128]{0,1:T(8,128)S(1)}, f32[128,128]{0,1:T(8,128)S(1)}) %tuple.48), branch_computations={%region_15.18_spmd, %region_16.19_spmd} | conditional | flops 3799552 | bytes 8757640 | solution.py:187
  41.3 0.2 multiply_subtract_fusion.2
  41.5 0.2 multiply_subtract_fusion.3
  42.1 0.4 multiply_subtract_fusion
  42.5 0.3 multiply_subtract_fusion.1
  42.8 0.2 fusion.33
  43.3 3.2 %conditional.5 = (f32[3,128,128]{2,1,0:T(8,128)S(1)}) conditional(s32[]{:T(128)} %convert_element_type.17, () %tuple.49, (f32[3,132,258]{2,1,0:T(8,128)S(1)}, f32[132,132]{1,0:T(8,128)S(1)}, f32[128,128]{0,1:T(8,128)S(1)}, f32[128,128]{0,1:T(8,128)S(1)}) %tuple.50), branch_computations={%region_18.21_spmd, %region_19.22_spmd} | conditional | flops 3799552 | bytes 8757640 | solution.py:187
  43.5 0.2 slice_bitcast_fusion.10
  44.5 0.2 multiply_subtract_fusion.6
  44.7 0.2 multiply_subtract_fusion.7
  45.3 0.4 multiply_subtract_fusion.4
  45.7 0.3 multiply_subtract_fusion.5
  46.0 0.2 fusion.75
  46.7 1.9 %collective-permute-start.8 = (f32[3,128,2]{2,1,0:T(8,128)S(1)}, f32[3,128,2]{2,1,0:T(8,128)S(1)}, u32[]{:S(2)}, u32[]{:S(2)}) collective-permute-start(f32[3,128,2]{2,1,0:T(8,128)S(1)} %get-tuple-element.217), channel_id=1, source_target_pairs={{0,4},{4,8},{8,12},{12,16},{16,20},{20,24},{24,28},{1,5},{5,9},{9,... | collective-permute-start | bytes 9224 | tf_op jit(solution)/shard_map/ppermute | solution.py:23
  48.6 4.5 %collective-permute-start.9 = (f32[3,128,2]{2,1,0:T(8,128)S(1)}, f32[3,128,2]{2,1,0:T(8,128)S(1)}, u32[]{:S(2)}, u32[]{:S(2)}) collective-permute-start(f32[3,128,2]{2,1,0:T(8,128)S(1)} %get-tuple-element.218), channel_id=1, source_target_pairs={{4,0},{8,4},{12,8},{16,12},{20,16},{24,20},{28,24},{5,1},{9,5},{13... | collective-permute-start | bytes 9224 | tf_op jit(solution)/shard_map/ppermute | solution.py:24
  53.1 1.5 %collective-permute-done.8 = f32[3,128,2]{2,1,0:T(8,128)S(1)} collective-permute-done((f32[3,128,2]{2,1,0:T(8,128)S(1)}, f32[3,128,2]{2,1,0:T(8,128)S(1)}, u32[]{:S(2)}, u32[]{:S(2)}) %collective-permute-start.8) | collective-permute-done | bytes 3104 | tf_op jit(solution)/shard_map/ppermute | solution.py:23
  54.7 1.7 %collective-permute-done.9 = f32[3,128,2]{2,1,0:T(8,128)S(1)} collective-permute-done((f32[3,128,2]{2,1,0:T(8,128)S(1)}, f32[3,128,2]{2,1,0:T(8,128)S(1)}, u32[]{:S(2)}, u32[]{:S(2)}) %collective-permute-start.9) | collective-permute-done | bytes 3104 | tf_op jit(solution)/shard_map/ppermute | solution.py:24
  56.4 1.9 %collective-permute-start.10 = (f32[3,2,260]{2,1,0:T(2,128)S(1)}, f32[3,2,260]{2,1,0:T(2,128)S(1)}, u32[]{:S(2)}, u32[]{:S(2)}) collective-permute-start(f32[3,2,260]{2,1,0:T(2,128)S(1)} %get-tuple-element.201), channel_id=1, source_target_pairs={{0,1},{1,2},{2,3},{4,5},{5,6},{6,7},{8,9},{9,10},{10,11},{12,13},{... | collective-permute-start | bytes 18728 | tf_op jit(solution)/shard_map/ppermute | solution.py:23
  58.3 3.9 %collective-permute-start.11 = (f32[3,2,260]{2,1,0:T(2,128)S(1)}, f32[3,2,260]{2,1,0:T(2,128)S(1)}, u32[]{:S(2)}, u32[]{:S(2)}) collective-permute-start(f32[3,2,260]{2,1,0:T(2,128)S(1)} %get-tuple-element.202), channel_id=1, source_target_pairs={{1,0},{2,1},{3,2},{5,4},{6,5},{7,6},{9,8},{10,9},{11,10},{13,12},{... | collective-permute-start | bytes 18728 | tf_op jit(solution)/shard_map/ppermute | solution.py:24
  62.6 1.3 %collective-permute-done.11 = f32[3,2,260]{2,1,0:T(2,128)S(1)} collective-permute-done((f32[3,2,260]{2,1,0:T(2,128)S(1)}, f32[3,2,260]{2,1,0:T(2,128)S(1)}, u32[]{:S(2)}, u32[]{:S(2)}) %collective-permute-start.11) | collective-permute-done | bytes 6272 | tf_op jit(solution)/shard_map/ppermute | solution.py:24
  64.0 0.3 pad_maximum_fusion.3
  64.6 0.6 rev.50
  65.2 0.6 rev.51
  66.0 0.2 pad_maximum_fusion.4
  66.2 3.1 %conditional.6 = (f32[3,128,128]{2,1,0:T(8,128)S(1)}) conditional(s32[]{:T(128)} %convert_element_type.16, () %tuple.51, (f32[3,132,258]{2,1,0:T(8,128)S(1)}, f32[132,132]{1,0:T(8,128)S(1)}, f32[128,128]{0,1:T(8,128)S(1)}, f32[128,128]{0,1:T(8,128)S(1)}) %tuple.52), branch_computations={%region_20.23_spmd, %region_21.24_spmd} | conditional | flops 3799552 | bytes 8757640 | solution.py:187
  67.3 0.2 multiply_subtract_fusion.10
  67.5 0.2 multiply_subtract_fusion.11
  68.1 0.4 multiply_subtract_fusion.8
  68.5 0.3 multiply_subtract_fusion.9
  68.9 0.2 fusion.117
  69.3 3.2 %conditional.7 = (f32[3,128,128]{2,1,0:T(8,128)S(1)}) conditional(s32[]{:T(128)} %convert_element_type.17, () %tuple.53, (f32[3,132,258]{2,1,0:T(8,128)S(1)}, f32[132,132]{1,0:T(8,128)S(1)}, f32[128,128]{0,1:T(8,128)S(1)}, f32[128,128]{0,1:T(8,128)S(1)}) %tuple.54), branch_computations={%region_22.25_spmd, %region_23.26_spmd} | conditional | flops 3799552 | bytes 8757640 | solution.py:187
  69.5 0.2 slice_bitcast_fusion.22
  70.5 0.2 multiply_subtract_fusion.14
  70.7 0.2 multiply_subtract_fusion.15
  71.3 0.4 multiply_subtract_fusion.12
  71.7 0.3 multiply_subtract_fusion.13
  72.0 0.2 fusion.159
  72.5 0.9 %fusion.171 = f32[3,128,256]{2,1,0:T(8,128)} fusion(f32[3,128,256]{2,1,0:T(8,128)S(1)} %copy-done, f32[3,128,128]{2,1,0:T(8,128)S(1)} %get-tuple-element.254, f32[3,128,128]{2,1,0:T(8,128)S(1)} %get-tuple-element.253, f32[3,128,128]{2,1,0:T(8,128)S(1)} %get-tuple-element.252, f32[3,128,128]{2,1,0:T(8,128)S(1)} %get-tuple-element.251), kind=kLoop, calls=%fused_computation.403 | loop fusion | flops 786432 | bytes 1572864 | tf_op jit(solution)/shard_map/add | solution.py:255
  (127 shorter events, 9.1 us)
Async XLA Ops:
  1.0 21.4 %collective-permute-start.4 = (f32[128,4]{1,0:T(8,128)S(1)}, f32[128,4]{1,0:T(8,128)S(1)}, u32[]{:S(2)}, u32[]{:S(2)}) collective-permute-start(f32[128,4]{1,0:T(8,128)S(1)} %get-tuple-element.233), channel_id=1, source_target_pairs={{0,4},{4,8},{8,12},{12,16},{16,20},{20,24},{24,28},{1,5},{5,9},{9,... | collective-permute-start | bytes 6152 | tf_op jit(solution)/shard_map/ppermute | solution.py:23
  2.9 19.5 %collective-permute-start.5 = (f32[128,4]{1,0:T(8,128)S(1)}, f32[128,4]{1,0:T(8,128)S(1)}, u32[]{:S(2)}, u32[]{:S(2)}) collective-permute-start(f32[128,4]{1,0:T(8,128)S(1)} %get-tuple-element.234), channel_id=1, source_target_pairs={{4,0},{8,4},{12,8},{16,12},{20,16},{24,20},{28,24},{5,1},{9,5},{13... | collective-permute-start | bytes 6152 | tf_op jit(solution)/shard_map/ppermute | solution.py:24
  8.6 20.0 %collective-permute-start = (f32[3,128,2]{2,1,0:T(8,128)S(1)}, f32[3,128,2]{2,1,0:T(8,128)S(1)}, u32[]{:S(2)}, u32[]{:S(2)}) collective-permute-start(f32[3,128,2]{2,1,0:T(8,128)S(1)} %get-tuple-element.219), channel_id=1, source_target_pairs={{0,4},{4,8},{8,12},{12,16},{16,20},{20,24},{24,28},{1,5},{5,9},{9,... | collective-permute-start | bytes 9224 | tf_op jit(solution)/shard_map/ppermute | solution.py:23
  10.5 18.1 %collective-permute-start.1 = (f32[3,128,2]{2,1,0:T(8,128)S(1)}, f32[3,128,2]{2,1,0:T(8,128)S(1)}, u32[]{:S(2)}, u32[]{:S(2)}) collective-permute-start(f32[3,128,2]{2,1,0:T(8,128)S(1)} %get-tuple-element.220), channel_id=1, source_target_pairs={{4,0},{8,4},{12,8},{16,12},{20,16},{24,20},{28,24},{5,1},{9,5},{13... | collective-permute-start | bytes 9224 | tf_op jit(solution)/shard_map/ppermute | solution.py:24
  15.0 0.7 copy-start.5
  15.8 0.7 copy-start.6
  16.5 0.7 copy-start.4
  20.5 2.0 %copy-start.1 = (f32[128,256]{1,0:T(8,128)S(1)}, f32[128,256]{1,0:T(8,128)}, u32[]{:S(2)}) copy-start(f32[128,256]{1,0:T(8,128)} %param.31) | copy-start | bytes 393220
  20.5 8.1 %copy-start = (f32[3,128,256]{2,1,0:T(8,128)S(1)}, f32[3,128,256]{2,1,0:T(8,128)}, u32[]{:S(2)}) copy-start(f32[3,128,256]{2,1,0:T(8,128)} %param.30) | copy-start | bytes 1179652
  22.6 12.2 %collective-permute-start.7 = (f32[4,264]{1,0:T(4,128)S(1)}, f32[4,264]{1,0:T(4,128)S(1)}, u32[]{:S(2)}, u32[]{:S(2)}) collective-permute-start(f32[4,264]{1,0:T(4,128)S(1)} %get-tuple-element.221), channel_id=1, source_target_pairs={{1,0},{2,1},{3,2},{5,4},{6,5},{7,6},{9,8},{10,9},{11,10},{13,12},{... | collective-permute-start | bytes 12680 | tf_op jit(solution)/shard_map/ppermute | solution.py:24
  25.1 9.8 %collective-permute-start.6 = (f32[4,264]{1,0:T(4,128)S(1)}, f32[4,264]{1,0:T(4,128)S(1)}, u32[]{:S(2)}, u32[]{:S(2)}) collective-permute-start(f32[4,264]{1,0:T(4,128)S(1)} %get-tuple-element.222), channel_id=1, source_target_pairs={{0,1},{1,2},{2,3},{4,5},{5,6},{6,7},{8,9},{9,10},{10,11},{12,13},{... | collective-permute-start | bytes 12680 | tf_op jit(solution)/shard_map/ppermute | solution.py:23
  28.8 7.1 %collective-permute-start.2 = (f32[3,2,260]{2,1,0:T(2,128)S(1)}, f32[3,2,260]{2,1,0:T(2,128)S(1)}, u32[]{:S(2)}, u32[]{:S(2)}) collective-permute-start(f32[3,2,260]{2,1,0:T(2,128)S(1)} %get-tuple-element.203), channel_id=1, source_target_pairs={{0,1},{1,2},{2,3},{4,5},{5,6},{6,7},{8,9},{9,10},{10,11},{12,13},{... | collective-permute-start | bytes 18728 | tf_op jit(solution)/shard_map/ppermute | solution.py:23
  32.4 5.6 %collective-permute-start.3 = (f32[3,2,260]{2,1,0:T(2,128)S(1)}, f32[3,2,260]{2,1,0:T(2,128)S(1)}, u32[]{:S(2)}, u32[]{:S(2)}) collective-permute-start(f32[3,2,260]{2,1,0:T(2,128)S(1)} %get-tuple-element.204), channel_id=1, source_target_pairs={{1,0},{2,1},{3,2},{5,4},{6,5},{7,6},{9,8},{10,9},{11,10},{13,12},{... | collective-permute-start | bytes 18728 | tf_op jit(solution)/shard_map/ppermute | solution.py:24
  35.8 2.2 %copy-start.3 = (f32[3]{0:T(128)S(1)}, f32[3]{0:T(128)}, u32[]{:S(2)}) copy-start(f32[3]{0:T(128)} %constant.303.clone) | copy-start | bytes 40
  39.3 0.7 copy-start.2
  46.7 8.0 %collective-permute-start.8 = (f32[3,128,2]{2,1,0:T(8,128)S(1)}, f32[3,128,2]{2,1,0:T(8,128)S(1)}, u32[]{:S(2)}, u32[]{:S(2)}) collective-permute-start(f32[3,128,2]{2,1,0:T(8,128)S(1)} %get-tuple-element.217), channel_id=1, source_target_pairs={{0,4},{4,8},{8,12},{12,16},{16,20},{20,24},{24,28},{1,5},{5,9},{9,... | collective-permute-start | bytes 9224 | tf_op jit(solution)/shard_map/ppermute | solution.py:23
  48.6 7.7 %collective-permute-start.9 = (f32[3,128,2]{2,1,0:T(8,128)S(1)}, f32[3,128,2]{2,1,0:T(8,128)S(1)}, u32[]{:S(2)}, u32[]{:S(2)}) collective-permute-start(f32[3,128,2]{2,1,0:T(8,128)S(1)} %get-tuple-element.218), channel_id=1, source_target_pairs={{4,0},{8,4},{12,8},{16,12},{20,16},{24,20},{28,24},{5,1},{9,5},{13... | collective-permute-start | bytes 9224 | tf_op jit(solution)/shard_map/ppermute | solution.py:24
  56.4 6.1 %collective-permute-start.10 = (f32[3,2,260]{2,1,0:T(2,128)S(1)}, f32[3,2,260]{2,1,0:T(2,128)S(1)}, u32[]{:S(2)}, u32[]{:S(2)}) collective-permute-start(f32[3,2,260]{2,1,0:T(2,128)S(1)} %get-tuple-element.201), channel_id=1, source_target_pairs={{0,1},{1,2},{2,3},{4,5},{5,6},{6,7},{8,9},{9,10},{10,11},{12,13},{... | collective-permute-start | bytes 18728 | tf_op jit(solution)/shard_map/ppermute | solution.py:23
  58.3 5.6 %collective-permute-start.11 = (f32[3,2,260]{2,1,0:T(2,128)S(1)}, f32[3,2,260]{2,1,0:T(2,128)S(1)}, u32[]{:S(2)}, u32[]{:S(2)}) collective-permute-start(f32[3,2,260]{2,1,0:T(2,128)S(1)} %get-tuple-element.202), channel_id=1, source_target_pairs={{1,0},{2,1},{3,2},{5,4},{6,5},{7,6},{9,8},{10,9},{11,10},{13,12},{... | collective-permute-start | bytes 18728 | tf_op jit(solution)/shard_map/ppermute | solution.py:24
where the time goes:
time: 74.1 us; the launch traced here: 73.4 us
  starting transfers between devices  36.9 us (50%)
  other arithmetic  13.9 us (19%)
  local copies, waits for them, and re-layouts  13.4 us (18%)
  waiting for transfers between devices  6.56 us (9%)
  between operations  1.78 us (2%)
  loops' own time  0.83 us (1%)
    ppermute x6, starting transfers between devices, with_halo(): after = lax.ppermute(initial, axis, down)  22.3 us
    ppermute x6, starting transfers between devices, with_halo(): before = lax.ppermute(last, axis, up)  14.6 us
    ppermute x6, waiting for transfers between devices, with_halo(): after = lax.ppermute(initial, axis, down)  5.03 us
    sub x16, other arithmetic, rusanov_flux(): 0.5 * (a + b) - 0.5 * fastest * (r - l)  4.51 us
    slice x3, local copies, waits for them, and re-layouts, with_halo(): last = lax.slice_in_dim(x, length - width, length, axis=dim)  2.19 us
    unnamed x14, local copies, waits for them, and re-layouts  1.97 us
    sub x16, other arithmetic, face_states(): cut_along(field, 1, interior + 4, axis)  1.88 us
    select_n x24, other arithmetic, minmod_limit(): jnp.where(lower * upper > 0.0, jnp.sign(lower) * jnp.minimum(jnp.abs(lowe...  1.76 us
  transfers between devices with their start and end apart: 12, of which 4 were waited for; matrix products, arithmetic and copies ran while one was open for 10% of the time, Pallas kernels for 0%

commit v1 on v0

v1 whole, which is shorter than its diff:
```python
from functools import partial

import jax
import jax.numpy as jnp
from jax import lax
from jax.experimental import pallas as pl
from jax.experimental.pallas import tpu as pltpu
from jax.sharding import PartitionSpec as P

GRAVITY = 9.81
SPACING = 2.0
TIME_STEP = 0.1
MANNING = (0.03, 0.06, 0.1, 0.15)
MESH = pl.DeviceIdType.MESH
RIM = 4
PAD = 16
LANES = 128
ROWS = 8
GROUP = 4 * RIM


def minmod(a, b):
    return jnp.maximum(jnp.minimum(a, b), jnp.minimum(jnp.maximum(a, b), 0.0))


def physical(h, p, r):
    root = lax.rsqrt(h)
    u = p * (root * root)
    speed = jnp.abs(u) + (GRAVITY**0.5) * (h * root)
    return p * u + (0.5 * GRAVITY) * (h * h), r * u, speed


def twice_flux(left, right):
    l1, l2, lc = physical(*left)
    r1, r2, rc = physical(*right)
    c = jnp.maximum(lc, rc)
    return (
        (left[1] + right[1]) - c * (right[0] - left[0]),
        (l1 + r1) - c * (right[1] - left[1]),
        (l2 + r2) - c * (right[2] - left[2]),
    )


def after(x):
    return pltpu.roll(x, x.shape[1] - 1, 1)


def before(x):
    return pltpu.roll(x, 1, 1)


def lane_ids(shape):
    return lax.broadcasted_iota(jnp.int32, shape, 1)


def column_change(h, p, r):
    lefts, rights = [], []
    for v in (h, p, r):
        low = v - before(v)
        half = 0.5 * minmod(low, after(low))
        lefts.append(v + half)
        rights.append(after(v - half))
    return tuple(f - before(f) for f in twice_flux(lefts, rights))


def shifted(ref, f, start, width, moves):
    tall = ref[f, pl.ds(start - 8, ROWS + 16), :width]
    return [tall[8 + k : 8 + k + ROWS] for k in moves]


def row_fluxes(ref, start, width):
    lefts, rights = [], []
    for f in (0, 2, 1):
        a, b, c, d = shifted(ref, f, start, width, (-1, 0, 1, 2))
        ab, bc, cd = b - a, c - b, d - c
        lefts.append(b + 0.5 * minmod(ab, bc))
        rights.append(c - 0.5 * minmod(bc, cd))
    return twice_flux(lefts, rights)


def friction_of(level):
    value = jnp.float32(0.0)
    for number, n in enumerate(MANNING):
        value = jnp.where(level == number, jnp.float32(n * n), value)
    return value


def kernel(
    size,
    water,
    bed,
    active,
    roughness,
    out,
    fields,
    section,
    fluxes,
    slopes,
    scales,
    row_out,
    row_in,
    col_out,
    col_in,
    corner_in,
    load_sem,
    send_sem,
    recv_sem,
):
    rows, cols, n_rows, n_cols = size
    ring = cols + LANES
    a, b = lax.axis_index("gy"), lax.axis_index("gx")
    has_up, has_down, has_left, has_right = a > 0, a < n_rows - 1, b > 0, b < n_cols - 1
    first, last = PAD, PAD + rows

    load_water = pltpu.make_async_copy(
        water, fields.at[0:3, first:last, 0:cols], load_sem.at[0]
    )
    load_bed = pltpu.make_async_copy(bed, fields.at[3, first:last, 0:cols], load_sem.at[1])
    load_water.start()
    load_bed.start()

    barrier = pltpu.get_barrier_semaphore()
    around = (
        (has_up, -1, 0),
        (has_down, 1, 0),
        (has_left, 0, -1),
        (has_right, 0, 1),
        (has_up & has_left, -1, -1),
        (has_up & has_right, -1, 1),
        (has_down & has_left, 1, -1),
        (has_down & has_right, 1, 1),
    )
    for there, da, db in around:

        @pl.when(there)
        def _(da=da, db=db):
            pl.semaphore_signal(
                barrier, inc=1, device_id={"gy": a + da, "gx": b + db}, device_id_type=MESH
            )

    lanes = lane_ids((8, LANES))
    tiles = cols // rows
    n_tile_rows, n_tile_cols = active.shape[1], active.shape[2]

    def tile_factors(row, col):
        row = jnp.clip(row, 0, n_tile_rows - 1)
        col = jnp.clip(col, 0, n_tile_cols - 1)
        on = TIME_STEP * active[0, row, col].astype(jnp.float32)
        return -on / (2.0 * SPACING), -GRAVITY * on * friction_of(roughness[row, col])

    for place, row in enumerate((a - 1, a, a + 1)):
        for t in range(tiles):
            for kind, value in enumerate(tile_factors(row, b * tiles + t)):
                scales[place, kind, :, t * rows : (t + 1) * rows] = jnp.full((8, rows), value)
        right = tile_factors(row, (b + 1) * tiles)
        left = tile_factors(row, b * tiles - 1)
        for kind in range(2):
            scales[place, kind, :, cols:] = jnp.where(
                lanes < LANES // 2, right[kind], left[kind]
            )

    load_water.wait()
    load_bed.wait()

    for f in range(4):
        row_out[0, f * RIM : (f + 1) * RIM, :] = fields[f, first : first + RIM, 0:cols]
        row_out[1, f * RIM : (f + 1) * RIM, :] = fields[f, last - RIM : last, 0:cols]
    per_reg = LANES // GROUP
    blocks = rows // 8
    for side, (lane0, shift0) in enumerate(((0, 0), (cols - LANES, RIM))):
        for reg in range(blocks // per_reg):
            total = jnp.zeros((8, LANES), jnp.float32)
            for j in range(per_reg):
                row0 = first + 8 * (reg * per_reg + j)
                for f in range(4):
                    at = GROUP * j + RIM * f
                    v = fields[f, row0 : row0 + 8, lane0 : lane0 + LANES]
                    shift = (at + shift0) % LANES
                    v = pltpu.roll(v, shift, 1) if shift else v
                    total = jnp.where((lanes >= at) & (lanes < at + RIM), v, total)
            col_out[side, 8 * reg : 8 * reg + 8, :] = total
    place = lanes % RIM
    sign = jnp.where((lanes // RIM) % 4 == 1, -1.0, 1.0)
    for side in range(2):
        for reg in range(blocks // per_reg):
            x = col_out[side, 8 * reg : 8 * reg + 8, :]
            flipped = pltpu.roll(x, 3, 1)
            for c, shift in ((2, 1), (1, LANES - 1), (0, LANES - 3)):
                flipped = jnp.where(place == c, pltpu.roll(x, shift, 1), flipped)
            col_out[2 + side, 8 * reg : 8 * reg + 8, :] = flipped * sign

    pl.semaphore_wait(
        barrier,
        (1 + has_up.astype(jnp.int32) + has_down.astype(jnp.int32))
        * (1 + has_left.astype(jnp.int32) + has_right.astype(jnp.int32))
        - 1,
    )

    top = slice(0, 8)
    bottom = slice(rows // per_reg - 8, rows // per_reg)
    row_slots = lambda k: row_in.at[k]
    transfers = []

    def send(there, src, dst, slot, da, db):
        number = len(transfers)
        copy = pltpu.make_async_remote_copy(
            src_ref=src,
            dst_ref=dst,
            send_sem=send_sem.at[number],
            recv_sem=recv_sem.at[slot],
            device_id={"gy": a + da, "gx": b + db},
            device_id_type=MESH,
        )
        transfers.append((there, copy))

        @pl.when(there)
        def _():
            copy.start()

    send(has_down, row_out.at[1], row_slots(0), 0, 1, 0)
    send(has_up, row_out.at[0], row_slots(1), 1, -1, 0)
    send(has_right, col_out.at[1], col_in.at[0], 2, 0, 1)
    send(has_left, col_out.at[0], col_in.at[1], 3, 0, -1)
    send(has_down & has_right, col_out.at[1, bottom], corner_in.at[0], 4, 1, 1)
    send(has_down & has_left, col_out.at[0, bottom], corner_in.at[1], 5, 1, -1)
    send(has_up & has_right, col_out.at[1, top], corner_in.at[2], 6, -1, 1)
    send(has_up & has_left, col_out.at[0, top], corner_in.at[3], 7, -1, -1)
    no_left, no_right = b == 0, b == n_cols - 1
    send(has_down & no_left, col_out.at[2, bottom], corner_in.at[0], 4, 1, 0)
    send(has_down & no_right, col_out.at[3, bottom], corner_in.at[1], 5, 1, 0)
    send(has_up & no_left, col_out.at[2, top], corner_in.at[2], 6, -1, 0)
    send(has_up & no_right, col_out.at[3, top], corner_in.at[3], 7, -1, 0)

    def arrive(there, dst, slot):
        @pl.when(there)
        def _():
            pltpu.make_async_remote_copy(
                src_ref=dst,
                dst_ref=dst,
                send_sem=send_sem.at[0],
                recv_sem=recv_sem.at[slot],
                device_id={"gy": a, "gx": b},
                device_id_type=MESH,
            ).wait_recv()

    @pl.when(no_left)
    def _():
        col_in[0] = col_out[2]

    @pl.when(no_right)
    def _():
        col_in[1] = col_out[3]

    arrive(has_left, col_in.at[0], 2)
    arrive(has_right, col_in.at[1], 3)

    def unpack(left, right, j, f):
        at = GROUP * j + RIM * f
        right = pltpu.roll(right, (LANES - at) % LANES, 1) if at else right
        left = pltpu.roll(left, (2 * LANES - RIM - at) % LANES, 1)
        return jnp.where(lanes < LANES // 2, right, left)

    for reg in range(blocks // per_reg):
        left = col_in[0, 8 * reg : 8 * reg + 8, :]
        right = col_in[1, 8 * reg : 8 * reg + 8, :]
        for j in range(per_reg):
            row0 = first + 8 * (reg * per_reg + j)
            for f in range(4):
                fields[f, row0 : row0 + 8, cols:] = unpack(left, right, j, f)

    arrive(has_up, row_in.at[0], 0)
    arrive(has_up, corner_in.at[0], 4)
    arrive(has_up, corner_in.at[1], 5)
    arrive(has_down, row_in.at[1], 1)
    arrive(has_down, corner_in.at[2], 6)
    arrive(has_down, corner_in.at[3], 7)

    @pl.when(has_up)
    def _():
        for f in range(4):
            fields[f, first - 8 : first, cols:] = unpack(
                corner_in[0], corner_in[1], per_reg - 1, f
            )
            fields[f, first - RIM : first, 0:cols] = row_in[0, f * RIM : (f + 1) * RIM, :]

    @pl.when(has_down)
    def _():
        for f in range(4):
            fields[f, last : last + 8, cols:] = unpack(corner_in[2], corner_in[3], 0, f)
            fields[f, last : last + RIM, 0:cols] = row_in[1, f * RIM : (f + 1) * RIM, :]

    @pl.when(jnp.logical_not(has_up))
    def _():
        for f in range(4):
            for k in range(RIM):
                v = fields[f, first + k : first + k + 1, :]
                fields[f, first - 1 - k : first - k, :] = -v if f == 2 else v

    @pl.when(jnp.logical_not(has_down))
    def _():
        for f in range(4):
            for k in range(RIM):
                v = fields[f, last - 1 - k : last - k, :]
                fields[f, last + k : last + k + 1, :] = -v if f == 2 else v

    def flux_block(ref, start, width):
        for f, flux in enumerate(row_fluxes(ref, start, width)):
            fluxes[f, pl.ds(start, ROWS), :width] = flux

    def change(ref, start, width, place, gx, gy):
        h, p, r = (ref[f, pl.ds(start, ROWS), :] for f in range(3))
        x0, x1, x2 = (v[:, :width] for v in column_change(h, p, r))
        h, p, r = (v[:, :width] for v in (h, p, r))
        y0, y1, y2 = (
            below - above
            for below, above in (shifted(fluxes, f, start, width, (0, -1)) for f in range(3))
        )
        scale = scales[place, 0, :ROWS, :width]
        drag = scales[place, 1, :ROWS, :width]
        drag = drag * (jnp.sqrt(p * p + r * r) * jnp.exp(jnp.log(h) * (-7.0 / 3.0)))
        return (
            (h, p, r),
            (
                scale * (x0 + y0),
                scale * (x1 + y2 + h * gx) + drag * p,
                scale * (x2 + y1 + h * gy) + drag * r,
            ),
        )

    def first_block(start, place):
        level = fields[3, pl.ds(start, ROWS), :]
        gx = GRAVITY * (after(level) - before(level))
        south, north = shifted(fields, 3, start, ring, (1, -1))
        gy = GRAVITY * (south - north)
        slopes[0, pl.ds(start, ROWS), :] = gx
        slopes[1, pl.ds(start, ROWS), :] = gy
        state, rates = change(fields, start, ring, place, gx, gy)
        for f in range(3):
            section[f, pl.ds(start, ROWS), :] = state[f] + rates[f]

    def second_block(start):
        gx = slopes[0, pl.ds(start, ROWS), :cols]
        gy = slopes[1, pl.ds(start, ROWS), :cols]
        state, rates = change(section, start, cols, 1, gx, gy)
        for f in range(3):
            out[f, pl.ds(start - first, ROWS), :] = 0.5 * (
                fields[f, pl.ds(start, ROWS), :cols] + (state[f] + rates[f])
            )

    def each(begin, finish, work):
        def step(i, carry):
            work(pl.multiple_of(i * ROWS, 8))
            return carry

        lax.fori_loop(begin // ROWS, finish // ROWS, step, 0)

    each(first - 8, last + 8, lambda s: flux_block(fields, s, ring))
    first_block(first - 8, 0)
    each(first, last, lambda s: first_block(s, 1))
    first_block(last, 2)
    each(first - 8, last, lambda s: flux_block(section, s, cols))
    each(first, last, second_block)

    for there, copy in transfers:

        @pl.when(there)
        def _(copy=copy):
            copy.wait_send()


def body(n_rows, n_cols, water_state, bed_level, active_tiles, roughness):
    rows, cols = bed_level.shape
    ring, tall = cols + LANES, rows + 2 * PAD
    packed = rows * GROUP // LANES
    return pl.pallas_call(
        partial(kernel, (rows, cols, n_rows, n_cols)),
        out_shape=jax.ShapeDtypeStruct(water_state.shape, jnp.float32),
        in_specs=[
            pl.BlockSpec(memory_space=pl.ANY),
            pl.BlockSpec(memory_space=pl.ANY),
            pl.BlockSpec(memory_space=pltpu.SMEM),
            pl.BlockSpec(memory_space=pltpu.SMEM),
        ],
        out_specs=pl.BlockSpec(memory_space=pltpu.VMEM),
        scratch_shapes=[
            pltpu.VMEM((4, tall, ring), jnp.float32),
            pltpu.VMEM((3, tall, ring), jnp.float32),
            pltpu.VMEM((3, tall, ring), jnp.float32),
            pltpu.VMEM((2, tall, ring), jnp.float32),
            pltpu.VMEM((3, 2, 8, ring), jnp.float32),
            pltpu.VMEM((2, 4 * RIM, cols), jnp.float32),
            pltpu.VMEM((2, 4 * RIM, cols), jnp.float32),
            pltpu.VMEM((4, packed, LANES), jnp.float32),
            pltpu.VMEM((2, packed, LANES), jnp.float32),
            pltpu.VMEM((4, 8, LANES), jnp.float32),
            pltpu.SemaphoreType.DMA((2,)),
            pltpu.SemaphoreType.DMA((12,)),
            pltpu.SemaphoreType.DMA((8,)),
        ],
        compiler_params=pltpu.CompilerParams(
            collective_id=0, has_side_effects=True, vmem_limit_bytes=32 * 1024 * 1024
        ),
        cost_estimate=pl.CostEstimate(
            flops=400 * 3 * rows * cols, bytes_accessed=32 * rows * cols, transcendentals=0
        ),
    )(water_state, bed_level, active_tiles, roughness)


def solution(mesh):
    return jax.shard_map(
        partial(body, mesh.shape["gy"], mesh.shape["gx"]),
        mesh=mesh,
        in_specs=(P(None, "gy", "gx"), P("gy", "gx"), P(), P()),
        out_specs=P(None, "gy", "gx"),
        check_vma=False,
    )
```

time: 74.1 us -> 24.9 us (0.34)
  the two profiles are of different devices: /device:TPU:12 before, /device:TPU:0 now
where the time goes in v1:
time: 24.9 us; the launch traced here: 24.7 us
  Pallas kernels  20.7 us (83%)
  local copies, waits for them, and re-layouts  4.01 us (16%)
    pallas_call x1, Pallas kernels, body(): pl.pallas_call(partial(kernel, (rows, cols, n_rows, n_cols)), out_shape=j...  20.7 us
    unnamed x9, local copies, waits for them, and re-layouts  4.01 us

profile of v1, /device:TPU:0, one launch (start us, length us, event | category | flops | bytes accessed | tf_op | source)
XLA Modules:
  0.0 24.7 jit_solution(996016017789758953)
XLA Ops:
  0.0 0.0 copy-start
  0.0 1.0 %copy-done = f32[3,128,256]{2,1,0:T(8,128)S(1)} copy-done((f32[3,128,256]{2,1,0:T(8,128)S(1)}, f32[3,128,256]{2,1,0:T(8,128)}, u32[]{:S(2)}) %copy-start) | copy-done | bytes 393240
  1.0 0.0 copy-start.1
  1.0 0.9 %copy-done.1 = f32[128,256]{1,0:T(8,128)S(1)} copy-done((f32[128,256]{1,0:T(8,128)S(1)}, f32[128,256]{1,0:T(8,128)}, u32[]{:S(2)}) %copy-start.1) | copy-done | bytes 131096
  1.9 0.0 copy-start.2
  1.9 0.7 %copy-done.2 = s32[1,4,16]{2,1,0:T(4,128)S(1)} copy-done((s32[1,4,16]{2,1,0:T(4,128)S(1)}, s32[1,4,16]{2,1,0:T(4,128)}, u32[]{:S(2)}) %copy-start.2) | copy-done | bytes 280
  2.6 0.0 copy-start.3
  2.6 0.7 %copy-done.3 = s32[4,16]{1,0:T(4,128)S(1)} copy-done((s32[4,16]{1,0:T(4,128)S(1)}, s32[4,16]{1,0:T(4,128)}, u32[]{:S(2)}) %copy-start.3) | copy-done | bytes 280
  3.3 20.7 %shard_map.46 = f32[3,128,256]{2,1,0:T(8,128)S(1)} custom-call(f32[3,128,256]{2,1,0:T(8,128)S(1)} %copy-done, f32[128,256]{1,0:T(8,128)S(1)} %copy-done.1, s32[1,4,16]{2,1,0:T(4,128)S(1)} %copy-done.2, s32[4,16]{1,0:T(4,128)S(1)} %copy-done.3), custom_call_target="tpu_custom_call" | custom-call | flops 39321600 | bytes 1048576 | tf_op jit(solution)/shard_map/pallas_call | solution.py:375
  24.0 0.7 %copy.6 = f32[3,128,256]{2,1,0:T(8,128)} copy(f32[3,128,256]{2,1,0:T(8,128)S(1)} %shard_map.46) | data formatting | bytes 786432
Async XLA Ops:
  0.0 1.0 %copy-start = (f32[3,128,256]{2,1,0:T(8,128)S(1)}, f32[3,128,256]{2,1,0:T(8,128)}, u32[]{:S(2)}) copy-start(f32[3,128,256]{2,1,0:T(8,128)} %water.1) | copy-start | bytes 1179652
  1.0 0.9 %copy-start.1 = (f32[128,256]{1,0:T(8,128)S(1)}, f32[128,256]{1,0:T(8,128)}, u32[]{:S(2)}) copy-start(f32[128,256]{1,0:T(8,128)} %bed.1) | copy-start | bytes 393220
  1.9 0.7 %copy-start.2 = (s32[1,4,16]{2,1,0:T(4,128)S(1)}, s32[1,4,16]{2,1,0:T(4,128)}, u32[]{:S(2)}) copy-start(s32[1,4,16]{2,1,0:T(4,128)} %active.1) | copy-start | bytes 772
  2.6 0.7 %copy-start.3 = (s32[4,16]{1,0:T(4,128)S(1)}, s32[4,16]{1,0:T(4,128)}, u32[]{:S(2)}) copy-start(s32[4,16]{1,0:T(4,128)} %roughness.1) | copy-start | bytes 772

commit v2 on v1

v2 whole, which is shorter than its diff:
```python
from functools import partial

import jax
import jax.numpy as jnp
from jax import lax
from jax.experimental import pallas as pl
from jax.experimental.pallas import tpu as pltpu
from jax.sharding import PartitionSpec as P

GRAVITY = 9.81
SPACING = 2.0
TIME_STEP = 0.1
MANNING = (0.03, 0.06, 0.1, 0.15)
MESH = pl.DeviceIdType.MESH
RIM = 4
PAD = 16
LANES = 128
STEP = 4
GROUP = 4 * RIM


def minmod(a, b):
    return jnp.maximum(jnp.minimum(a, b), jnp.minimum(jnp.maximum(a, b), 0.0))


def physical(h, p, r):
    root = lax.rsqrt(h)
    u = p * (root * root)
    speed = jnp.abs(u) + (GRAVITY**0.5) * (h * root)
    return p * u + (0.5 * GRAVITY) * (h * h), r * u, speed


def twice_flux(left, right):
    l1, l2, lc = physical(*left)
    r1, r2, rc = physical(*right)
    c = jnp.maximum(lc, rc)
    return (
        (left[1] + right[1]) - c * (right[0] - left[0]),
        (l1 + r1) - c * (right[1] - left[1]),
        (l2 + r2) - c * (right[2] - left[2]),
    )


def moved(x, by):
    return pltpu.roll(x, (-by) % x.shape[-1], x.ndim - 1)


def lane_ids(shape):
    return lax.broadcasted_iota(jnp.int32, shape, len(shape) - 1)


def faces(a, b, c, d):
    ab, bc, cd = b - a, c - b, d - c
    return b + 0.5 * minmod(ab, bc), c - 0.5 * minmod(bc, cd)


def column_change(h, p, r):
    sides = [faces(moved(v, -1), v, moved(v, 1), moved(v, 2)) for v in (h, p, r)]
    flux = twice_flux([s[0] for s in sides], [s[1] for s in sides])
    return tuple(f - moved(f, -1) for f in flux)


def row_fluxes(h, p, r):
    n = h.shape[0]
    sides = [faces(v[: n - 3], v[1 : n - 2], v[2 : n - 1], v[3:]) for v in (h, r, p)]
    return twice_flux([s[0] for s in sides], [s[1] for s in sides])


def friction_of(level):
    value = jnp.float32(0.0)
    for number, n in enumerate(MANNING):
        value = jnp.where(level == number, jnp.float32(n * n), value)
    return value


def kernel(
    size,
    water,
    bed,
    active_hbm,
    roughness_hbm,
    out,
    active,
    roughness,
    fields,
    tiled,
    section,
    slopes,
    result,
    scales,
    row_out,
    row_in,
    col_out,
    col_in,
    corner_in,
    load_sem,
    send_sem,
    recv_sem,
):
    rows, cols, n_rows, n_cols = size
    ring = cols + LANES
    a, b = lax.axis_index("gy"), lax.axis_index("gx")
    has_up, has_down, has_left, has_right = a > 0, a < n_rows - 1, b > 0, b < n_cols - 1
    first, last = PAD, PAD + rows

    panels = cols // LANES
    load_active = pltpu.make_async_copy(active_hbm, active, load_sem.at[0])
    load_roughness = pltpu.make_async_copy(roughness_hbm, roughness, load_sem.at[1])
    loads = []
    for c in range(panels):
        part = pl.ds(c * LANES, LANES)
        for src, dst in (
            (water.at[:, :, part], fields.at[0:3, c, first:last, :]),
            (bed.at[:, part], fields.at[3, c, first:last, :]),
        ):
            loads.append(pltpu.make_async_copy(src, dst, load_sem.at[2 + len(loads)]))
    for load in (load_active, load_roughness, *loads):
        load.start()

    barrier = pltpu.get_barrier_semaphore()
    around = (
        (has_up, -1, 0),
        (has_down, 1, 0),
        (has_left, 0, -1),
        (has_right, 0, 1),
        (has_up & has_left, -1, -1),
        (has_up & has_right, -1, 1),
        (has_down & has_left, 1, -1),
        (has_down & has_right, 1, 1),
    )
    for there, da, db in around:

        @pl.when(there)
        def _(da=da, db=db):
            pl.semaphore_signal(
                barrier, inc=1, device_id={"gy": a + da, "gx": b + db}, device_id_type=MESH
            )

    load_active.wait()
    load_roughness.wait()
    lanes = lane_ids((8, LANES))
    tiles = cols // rows
    n_tile_rows, n_tile_cols = active.shape[1], active.shape[2]

    def tile_factors(row, col):
        row = jnp.clip(row, 0, n_tile_rows - 1)
        col = jnp.clip(col, 0, n_tile_cols - 1)
        on = TIME_STEP * active[0, row, col].astype(jnp.float32)
        return -on / (2.0 * SPACING), -GRAVITY * on * friction_of(roughness[row, col])

    sublanes = lax.broadcasted_iota(jnp.int32, (8, LANES), 0)
    for place, row in ((1, a), (0, a - 1), (2, a + 1)):
        parts = [tile_factors(row, b * tiles + t) for t in range(tiles)]
        right = tile_factors(row, (b + 1) * tiles)
        left = tile_factors(row, b * tiles - 1)
        for kind in range(2):
            values = [
                jnp.full((8, LANES), parts[lane0 // rows][kind]) for lane0 in range(0, cols, LANES)
            ]
            values.append(jnp.where(lanes < LANES // 2, right[kind], left[kind]))
            for k, value in enumerate(values):
                at = slice(k * LANES, (k + 1) * LANES)
                if place != 1:
                    other = sublanes == (0 if place == 0 else 7)
                    value = jnp.where(other, value, scales[1, kind, :, at])
                scales[place, kind, :, at] = value

    for load in loads:
        load.wait()

    for f in range(4):
        for c in range(panels):
            at = slice(c * LANES, (c + 1) * LANES)
            row_out[0, f * RIM : (f + 1) * RIM, at] = fields[f, c, first : first + RIM]
            row_out[1, f * RIM : (f + 1) * RIM, at] = fields[f, c, last - RIM : last]
    per_reg = LANES // GROUP
    blocks = rows // 8
    for side, (panel, shift0) in enumerate(((0, 0), (panels - 1, RIM))):
        for reg in range(blocks // per_reg):
            total = jnp.zeros((8, LANES), jnp.float32)
            for j in range(per_reg):
                row0 = first + 8 * (reg * per_reg + j)
                for f in range(4):
                    at = GROUP * j + RIM * f
                    v = fields[f, panel, row0 : row0 + 8]
                    shift = (at + shift0) % LANES
                    v = pltpu.roll(v, shift, 1) if shift else v
                    total = jnp.where((lanes >= at) & (lanes < at + RIM), v, total)
            col_out[side, 8 * reg : 8 * reg + 8, :] = total
    place = lanes % RIM
    sign = jnp.where((lanes // RIM) % 4 == 1, -1.0, 1.0)
    for side in range(2):
        for reg in range(blocks // per_reg):
            x = col_out[side, 8 * reg : 8 * reg + 8, :]
            flipped = pltpu.roll(x, 3, 1)
            for c, shift in ((2, 1), (1, LANES - 1), (0, LANES - 3)):
                flipped = jnp.where(place == c, pltpu.roll(x, shift, 1), flipped)
            col_out[2 + side, 8 * reg : 8 * reg + 8, :] = flipped * sign

    pl.semaphore_wait(
        barrier,
        (1 + has_up.astype(jnp.int32) + has_down.astype(jnp.int32))
        * (1 + has_left.astype(jnp.int32) + has_right.astype(jnp.int32))
        - 1,
    )

    top = slice(0, 8)
    bottom = slice(rows // per_reg - 8, rows // per_reg)
    row_slots = lambda k: row_in.at[k]
    transfers = []

    def send(there, src, dst, slot, da, db):
        number = len(transfers)
        copy = pltpu.make_async_remote_copy(
            src_ref=src,
            dst_ref=dst,
            send_sem=send_sem.at[number],
            recv_sem=recv_sem.at[slot],
            device_id={"gy": a + da, "gx": b + db},
            device_id_type=MESH,
        )
        transfers.append((there, copy))

        @pl.when(there)
        def _():
            copy.start()

    send(has_down, row_out.at[1], row_slots(0), 0, 1, 0)
    send(has_up, row_out.at[0], row_slots(1), 1, -1, 0)
    send(has_right, col_out.at[1], col_in.at[0], 2, 0, 1)
    send(has_left, col_out.at[0], col_in.at[1], 3, 0, -1)
    send(has_down & has_right, col_out.at[1, bottom], corner_in.at[0], 4, 1, 1)
    send(has_down & has_left, col_out.at[0, bottom], corner_in.at[1], 5, 1, -1)
    send(has_up & has_right, col_out.at[1, top], corner_in.at[2], 6, -1, 1)
    send(has_up & has_left, col_out.at[0, top], corner_in.at[3], 7, -1, -1)
    no_left, no_right = b == 0, b == n_cols - 1
    send(has_down & no_left, col_out.at[2, bottom], corner_in.at[0], 4, 1, 0)
    send(has_down & no_right, col_out.at[3, bottom], corner_in.at[1], 5, 1, 0)
    send(has_up & no_left, col_out.at[2, top], corner_in.at[2], 6, -1, 0)
    send(has_up & no_right, col_out.at[3, top], corner_in.at[3], 7, -1, 0)

    def arrive(there, dst, slot):
        @pl.when(there)
        def _():
            pltpu.make_async_remote_copy(
                src_ref=dst,
                dst_ref=dst,
                send_sem=send_sem.at[0],
                recv_sem=recv_sem.at[slot],
                device_id={"gy": a, "gx": b},
                device_id_type=MESH,
            ).wait_recv()

    @pl.when(no_left)
    def _():
        col_in[0] = col_out[2]

    @pl.when(no_right)
    def _():
        col_in[1] = col_out[3]

    arrive(has_left, col_in.at[0], 2)
    arrive(has_right, col_in.at[1], 3)

    def unpack(left, right, j, f):
        at = GROUP * j + RIM * f
        right = pltpu.roll(right, (LANES - at) % LANES, 1) if at else right
        left = pltpu.roll(left, (2 * LANES - RIM - at) % LANES, 1)
        return jnp.where(lanes < LANES // 2, right, left)

    for reg in range(blocks // per_reg):
        left = col_in[0, 8 * reg : 8 * reg + 8, :]
        right = col_in[1, 8 * reg : 8 * reg + 8, :]
        for j in range(per_reg):
            row0 = first + 8 * (reg * per_reg + j)
            for f in range(4):
                fields[f, panels, row0 : row0 + 8] = unpack(left, right, j, f)

    arrive(has_up, row_in.at[0], 0)
    arrive(has_up, corner_in.at[0], 4)
    arrive(has_up, corner_in.at[1], 5)
    arrive(has_down, row_in.at[1], 1)
    arrive(has_down, corner_in.at[2], 6)
    arrive(has_down, corner_in.at[3], 7)

    @pl.when(has_up)
    def _():
        for f in range(4):
            fields[f, panels, first - 8 : first] = unpack(
                corner_in[0], corner_in[1], per_reg - 1, f
            )
            for c in range(panels):
                fields[f, c, first - RIM : first] = row_in[
                    0, f * RIM : (f + 1) * RIM, c * LANES : (c + 1) * LANES
                ]

    @pl.when(has_down)
    def _():
        for f in range(4):
            fields[f, panels, last : last + 8] = unpack(corner_in[2], corner_in[3], 0, f)
            for c in range(panels):
                fields[f, c, last : last + RIM] = row_in[
                    1, f * RIM : (f + 1) * RIM, c * LANES : (c + 1) * LANES
                ]

    @pl.when(jnp.logical_not(has_up))
    def _():
        for f in range(4):
            for k in range(RIM):
                v = fields[f, :, first + k : first + k + 1]
                fields[f, :, first - 1 - k : first - k] = -v if f == 2 else v

    @pl.when(jnp.logical_not(has_down))
    def _():
        for f in range(4):
            for k in range(RIM):
                v = fields[f, :, last - 1 - k : last - k]
                fields[f, :, last + k : last + k + 1] = -v if f == 2 else v

    stride = rows // 8

    for t in range(-RIM, stride + RIM):
        for f in range(4):
            for c in range(panels + 1):
                tiled[f, t + RIM, :, c * LANES : (c + 1) * LANES] = fields[
                    f, c, pl.ds(first + t, 8, stride), :
                ]

    def tiles_of(ref, f, t, count, origin, width):
        return ref[f, pl.ds(t + origin, count), :, :width]

    def fluxes_at(ref, t, count, origin, width):
        return row_fluxes(
            *(tiles_of(ref, f, t - 1, count + 3, origin, width) for f in range(3))
        )

    def section_rates(ref, t, count, origin, width, carry, scale, drag, gx, gy):
        h, p, r = (tiles_of(ref, f, t, count, origin, ring) for f in range(3))
        x0, x1, x2 = (v[..., :width] for v in column_change(h, p, r))
        h, p, r = (v[..., :width] for v in (h, p, r))
        below = fluxes_at(ref, t, count, origin, width)
        y0, y1, y2 = (
            now - jnp.concatenate([last_one, now[:-1]], axis=0)
            for now, last_one in zip(below, carry)
        )
        drag = drag * (jnp.sqrt(p * p + r * r) * jnp.exp(jnp.log(h) * (-7.0 / 3.0)))
        state = (
            h + scale * (x0 + y0),
            p + (scale * (x1 + y2 + h * gx) + drag * p),
            r + (scale * (x2 + y1 + h * gy) + drag * r),
        )
        return state, tuple(flux[-1:] for flux in below)

    def first_tiles(t, count, place, carry):
        level = tiles_of(tiled, 3, t, count, RIM, ring)
        gx = GRAVITY * (moved(level, 1) - moved(level, -1))
        gy = GRAVITY * (
            tiles_of(tiled, 3, t + 1, count, RIM, ring)
            - tiles_of(tiled, 3, t - 1, count, RIM, ring)
        )
        slopes[0, pl.ds(t + 2, count)] = gx
        slopes[1, pl.ds(t + 2, count)] = gy
        scale, drag = scales[place, 0][None], scales[place, 1][None]
        state, carry = section_rates(
            tiled, t, count, RIM, ring, carry, scale, drag, gx, gy
        )
        for f in range(3):
            section[f, pl.ds(t + 2, count)] = state[f]
        return carry

    def second_tiles(t, count, carry):
        gx = slopes[0, pl.ds(t + 2, count), :, :cols]
        gy = slopes[1, pl.ds(t + 2, count), :, :cols]
        scale, drag = scales[1, 0, :, :cols][None], scales[1, 1, :, :cols][None]
        state, carry = section_rates(
            section, t, count, 2, cols, carry, scale, drag, gx, gy
        )
        for f in range(3):
            final = 0.5 * (tiles_of(tiled, f, t, count, RIM, cols) + state[f])
            for k in range(count):
                for c in range(panels):
                    result[f, c, pl.ds(t + k, 8, stride), :] = final[
                        k, :, c * LANES : (c + 1) * LANES
                    ]
        return carry

    carry = fluxes_at(tiled, -3, 1, RIM, ring)
    carry = first_tiles(-2, 2, 0, carry)
    carry = lax.fori_loop(
        0, stride // STEP, lambda i, c: first_tiles(i * STEP, STEP, 1, c), carry
    )
    first_tiles(stride, 2, 2, carry)
    carry = fluxes_at(section, -1, 1, 2, cols)
    lax.fori_loop(0, stride // STEP, lambda i, c: second_tiles(i * STEP, STEP, c), carry)
    for c in range(panels):
        out[:, :, c * LANES : (c + 1) * LANES] = result[:, c]

    for there, copy in transfers:

        @pl.when(there)
        def _(copy=copy):
            copy.wait_send()


def body(n_rows, n_cols, water_state, bed_level, active_tiles, roughness):
    rows, cols = bed_level.shape
    ring, tall = cols + LANES, rows + 2 * PAD
    packed = rows * GROUP // LANES
    stride = rows // 8
    return pl.pallas_call(
        partial(kernel, (rows, cols, n_rows, n_cols)),
        out_shape=jax.ShapeDtypeStruct(water_state.shape, jnp.float32),
        in_specs=[
            pl.BlockSpec(memory_space=pltpu.HBM),
            pl.BlockSpec(memory_space=pltpu.HBM),
            pl.BlockSpec(memory_space=pltpu.HBM),
            pl.BlockSpec(memory_space=pltpu.HBM),
        ],
        out_specs=pl.BlockSpec(memory_space=pltpu.VMEM),
        scratch_shapes=[
            pltpu.SMEM(active_tiles.shape, jnp.int32),
            pltpu.SMEM(roughness.shape, jnp.int32),
            pltpu.VMEM((4, ring // LANES, tall, LANES), jnp.float32),
            pltpu.VMEM((4, stride + 2 * RIM, 8, ring), jnp.float32),
            pltpu.VMEM((3, stride + 4, 8, ring), jnp.float32),
            pltpu.VMEM((2, stride + 4, 8, ring), jnp.float32),
            pltpu.VMEM((3, cols // LANES, rows, LANES), jnp.float32),
            pltpu.VMEM((3, 2, 8, ring), jnp.float32),
            pltpu.VMEM((2, 4 * RIM, cols), jnp.float32),
            pltpu.VMEM((2, 4 * RIM, cols), jnp.float32),
            pltpu.VMEM((4, packed, LANES), jnp.float32),
            pltpu.VMEM((2, packed, LANES), jnp.float32),
            pltpu.VMEM((4, 8, LANES), jnp.float32),
            pltpu.SemaphoreType.DMA((2 + 2 * (cols // LANES),)),
            pltpu.SemaphoreType.DMA((12,)),
            pltpu.SemaphoreType.DMA((8,)),
        ],
        compiler_params=pltpu.CompilerParams(
            collective_id=0, has_side_effects=True, vmem_limit_bytes=24 * 1024 * 1024
        ),
        cost_estimate=pl.CostEstimate(
            flops=400 * 3 * rows * cols, bytes_accessed=32 * rows * cols, transcendentals=0
        ),
    )(water_state, bed_level, active_tiles, roughness)


def solution(mesh):
    return jax.shard_map(
        partial(body, mesh.shape["gy"], mesh.shape["gx"]),
        mesh=mesh,
        in_specs=(P(None, "gy", "gx"), P("gy", "gx"), P(), P()),
        out_specs=P(None, "gy", "gx"),
        check_vma=False,
    )
```

time: 24.9 us -> 15.5 us (0.62)
  Pallas kernels: 20.7 us -> 11.3 us
    pallas_call x1, Pallas kernels: 20.7 us -> 11.3 us  [body(): pl.pallas_call(partial(kernel, (rows, cols, n_rows, n_cols)), out_shape=j...]
where the time goes in v2:
time: 15.5 us; the launch traced here: 15.3 us
  Pallas kernels  11.3 us (73%)
  local copies, waits for them, and re-layouts  4.01 us (26%)
    pallas_call x1, Pallas kernels, body(): pl.pallas_call(partial(kernel, (rows, cols, n_rows, n_cols)), out_shape=j...  11.3 us
    unnamed x9, local copies, waits for them, and re-layouts  4.01 us

profile of v2, /device:TPU:0, one launch (start us, length us, event | category | flops | bytes accessed | tf_op | source)
XLA Modules:
  0.0 15.3 jit_solution(14745346158297960231)
XLA Ops:
  0.0 0.0 copy-start
  0.0 1.0 %copy-done = f32[3,128,256]{2,1,0:T(8,128)S(1)} copy-done((f32[3,128,256]{2,1,0:T(8,128)S(1)}, f32[3,128,256]{2,1,0:T(8,128)}, u32[]{:S(2)}) %copy-start) | copy-done | bytes 393240
  1.0 0.0 copy-start.1
  1.0 0.9 %copy-done.1 = f32[128,256]{1,0:T(8,128)S(1)} copy-done((f32[128,256]{1,0:T(8,128)S(1)}, f32[128,256]{1,0:T(8,128)}, u32[]{:S(2)}) %copy-start.1) | copy-done | bytes 131096
  1.9 0.0 copy-start.2
  1.9 0.7 %copy-done.2 = s32[1,4,16]{2,1,0:T(4,128)S(1)} copy-done((s32[1,4,16]{2,1,0:T(4,128)S(1)}, s32[1,4,16]{2,1,0:T(4,128)}, u32[]{:S(2)}) %copy-start.2) | copy-done | bytes 280
  2.6 0.0 copy-start.3
  2.6 0.7 %copy-done.3 = s32[4,16]{1,0:T(4,128)S(1)} copy-done((s32[4,16]{1,0:T(4,128)S(1)}, s32[4,16]{1,0:T(4,128)}, u32[]{:S(2)}) %copy-start.3) | copy-done | bytes 280
  3.3 11.3 %shard_map.46 = f32[3,128,256]{2,1,0:T(8,128)S(1)} custom-call(f32[3,128,256]{2,1,0:T(8,128)S(1)} %copy-done, f32[128,256]{1,0:T(8,128)S(1)} %copy-done.1, s32[1,4,16]{2,1,0:T(4,128)S(1)} %copy-done.2, s32[4,16]{1,0:T(4,128)S(1)} %copy-done.3), custom_call_target="tpu_custom_call" | custom-call | flops 39321600 | bytes 1048576 | tf_op jit(solution)/shard_map/pallas_call | solution.py:410
  14.6 0.7 %copy.6 = f32[3,128,256]{2,1,0:T(8,128)} copy(f32[3,128,256]{2,1,0:T(8,128)S(1)} %shard_map.46) | data formatting | bytes 786432
Async XLA Ops:
  0.0 1.0 %copy-start = (f32[3,128,256]{2,1,0:T(8,128)S(1)}, f32[3,128,256]{2,1,0:T(8,128)}, u32[]{:S(2)}) copy-start(f32[3,128,256]{2,1,0:T(8,128)} %water.1) | copy-start | bytes 1179652
  1.0 0.9 %copy-start.1 = (f32[128,256]{1,0:T(8,128)S(1)}, f32[128,256]{1,0:T(8,128)}, u32[]{:S(2)}) copy-start(f32[128,256]{1,0:T(8,128)} %bed.1) | copy-start | bytes 393220
  1.9 0.7 %copy-start.2 = (s32[1,4,16]{2,1,0:T(4,128)S(1)}, s32[1,4,16]{2,1,0:T(4,128)}, u32[]{:S(2)}) copy-start(s32[1,4,16]{2,1,0:T(4,128)} %active_hbm.1) | copy-start | bytes 772
  2.6 0.7 %copy-start.3 = (s32[4,16]{1,0:T(4,128)S(1)}, s32[4,16]{1,0:T(4,128)}, u32[]{:S(2)}) copy-start(s32[4,16]{1,0:T(4,128)} %roughness_hbm.1) | copy-start | bytes 772

commit v3 on v2

--- a/solution.py
+++ b/solution.py
@@ -392,8 +392,16 @@
     first_tiles(stride, 2, 2, carry)
     carry = fluxes_at(section, -1, 1, 2, cols)
     lax.fori_loop(0, stride // STEP, lambda i, c: second_tiles(i * STEP, STEP, c), carry)
+    stores = []
     for c in range(panels):
-        out[:, :, c * LANES : (c + 1) * LANES] = result[:, c]
+        stores.append(
+            pltpu.make_async_copy(
+                result.at[:, c], out.at[:, :, pl.ds(c * LANES, LANES)], load_sem.at[2 + c]
+            )
+        )
+        stores[-1].start()
+    for store in stores:
+        store.wait()
 
     for there, copy in transfers:
 
@@ -411,12 +419,12 @@
         partial(kernel, (rows, cols, n_rows, n_cols)),
         out_shape=jax.ShapeDtypeStruct(water_state.shape, jnp.float32),
         in_specs=[
-            pl.BlockSpec(memory_space=pltpu.HBM),
-            pl.BlockSpec(memory_space=pltpu.HBM),
-            pl.BlockSpec(memory_space=pltpu.HBM),
-            pl.BlockSpec(memory_space=pltpu.HBM),
+            pl.BlockSpec(memory_space=pl.ANY),
+            pl.BlockSpec(memory_space=pl.ANY),
+            pl.BlockSpec(memory_space=pl.ANY),
+            pl.BlockSpec(memory_space=pl.ANY),
         ],
-        out_specs=pl.BlockSpec(memory_space=pltpu.VMEM),
+        out_specs=pl.BlockSpec(memory_space=pl.ANY),
         scratch_shapes=[
             pltpu.SMEM(active_tiles.shape, jnp.int32),
             pltpu.SMEM(roughness.shape, jnp.int32),
@@ -436,7 +444,7 @@
             pltpu.SemaphoreType.DMA((8,)),
         ],
         compiler_params=pltpu.CompilerParams(
-            collective_id=0, has_side_effects=True, vmem_limit_bytes=24 * 1024 * 1024
+            collective_id=0, has_side_effects=True, vmem_limit_bytes=60 * 1024 * 1024
         ),
         cost_estimate=pl.CostEstimate(
             flops=400 * 3 * rows * cols, bytes_accessed=32 * rows * cols, transcendentals=0

time: 15.5 us -> 13.9 us (0.90)
  local copies, waits for them, and re-layouts: 4.01 us -> 1.77 us
  Pallas kernels: 11.3 us -> 11.9 us
    unnamed x9 -> x1, local copies, waits for them, and re-layouts: 4.01 us -> 1.77 us
    pallas_call x1, Pallas kernels: 11.3 us -> 11.9 us  [body(): pl.pallas_call(partial(kernel, (rows, cols, n_rows, n_cols)), out_shape=j...]
where the time goes in v3:
time: 13.9 us; the launch traced here: 13.7 us
  Pallas kernels  11.9 us (86%)
  local copies, waits for them, and re-layouts  1.77 us (13%)
    pallas_call x1, Pallas kernels, body(): pl.pallas_call(partial(kernel, (rows, cols, n_rows, n_cols)), out_shape=j...  11.9 us
    unnamed x1, local copies, waits for them, and re-layouts  1.77 us

profile of v3, /device:TPU:0, one launch (start us, length us, event | category | flops | bytes accessed | tf_op | source)
XLA Modules:
  0.0 13.7 jit_solution(1783860164750266383)
XLA Ops:
  0.0 11.9 %shard_map.46 = f32[3,128,256]{2,1,0:T(8,128)} custom-call(f32[3,128,256]{2,1,0:T(8,128)} %water.1, f32[128,256]{1,0:T(8,128)} %bed.1, s32[1,4,16]{2,1,0:T(4,128)} %active_hbm.1, s32[4,16]{1,0:T(4,128)} %roughness_hbm.1), custom_call_target="tpu_custom_call" | custom-call | flops 39321600 | bytes 1048576 | tf_op jit(solution)/shard_map/pallas_call | solution.py:418
  11.9 1.8 %copy.6 = f32[3,128,256]{2,1,0:T(8,128)} copy(f32[3,128,256]{2,1,0:T(8,128)} %shard_map.46) | data formatting | bytes 786432

commit v4 on v3

--- a/solution.py
+++ b/solution.py
@@ -85,6 +85,7 @@
     fields,
     tiled,
     section,
+    fluxes,
     slopes,
     result,
     scales,
@@ -239,6 +240,27 @@
     send(has_up & no_left, col_out.at[2, top], corner_in.at[2], 6, -1, 0)
     send(has_up & no_right, col_out.at[3, top], corner_in.at[3], 7, -1, 0)
 
+    stride = rows // 8
+
+    def retile(t, panel_range):
+        for f in range(4):
+            for c in panel_range:
+                tiled[f, t + RIM, :, c * LANES : (c + 1) * LANES] = fields[
+                    f, c, pl.ds(first + t, 8, stride), :
+                ]
+
+    def keep_fluxes(t, count, lane0, lane1):
+        values = row_fluxes(
+            *(tiled[f, pl.ds(t - 1 + RIM, count + 3), :, lane0:lane1] for f in range(3))
+        )
+        for f in range(3):
+            fluxes[f, pl.ds(t + 3, count), :, lane0:lane1] = values[f]
+
+    for t in range(stride):
+        retile(t, range(panels))
+    for t in range(1, stride - 2, STEP):
+        keep_fluxes(t, min(STEP, stride - 2 - t), 0, cols)
+
     def arrive(there, dst, slot):
         @pl.when(there)
         def _():
@@ -317,14 +339,9 @@
                 v = fields[f, :, last - 1 - k : last - k]
                 fields[f, :, last + k : last + k + 1] = -v if f == 2 else v
 
-    stride = rows // 8
 
     for t in range(-RIM, stride + RIM):
-        for f in range(4):
-            for c in range(panels + 1):
-                tiled[f, t + RIM, :, c * LANES : (c + 1) * LANES] = fields[
-                    f, c, pl.ds(first + t, 8, stride), :
-                ]
+        retile(t, range(panels, panels + 1) if 0 <= t < stride else range(panels + 1))
 
     def tiles_of(ref, f, t, count, origin, width):
         return ref[f, pl.ds(t + origin, count), :, :width]
@@ -338,7 +355,10 @@
         h, p, r = (tiles_of(ref, f, t, count, origin, ring) for f in range(3))
         x0, x1, x2 = (v[..., :width] for v in column_change(h, p, r))
         h, p, r = (v[..., :width] for v in (h, p, r))
-        below = fluxes_at(ref, t, count, origin, width)
+        if ref is tiled:
+            below = tuple(fluxes[f, pl.ds(t + 3, count)] for f in range(3))
+        else:
+            below = fluxes_at(ref, t, count, origin, width)
         y0, y1, y2 = (
             now - jnp.concatenate([last_one, now[:-1]], axis=0)
             for now, last_one in zip(below, carry)
@@ -384,7 +404,10 @@
                     ]
         return carry
 
-    carry = fluxes_at(tiled, -3, 1, RIM, ring)
+    keep_fluxes(-3, 4, 0, ring)
+    keep_fluxes(stride - 2, 4, 0, ring)
+    keep_fluxes(1, stride - 3, cols, ring)
+    carry = tuple(fluxes[f, pl.ds(0, 1)] for f in range(3))
     carry = first_tiles(-2, 2, 0, carry)
     carry = lax.fori_loop(
         0, stride // STEP, lambda i, c: first_tiles(i * STEP, STEP, 1, c), carry
@@ -431,6 +454,7 @@
             pltpu.VMEM((4, ring // LANES, tall, LANES), jnp.float32),
             pltpu.VMEM((4, stride + 2 * RIM, 8, ring), jnp.float32),
             pltpu.VMEM((3, stride + 4, 8, ring), jnp.float32),
+            pltpu.VMEM((3, stride + 5, 8, ring), jnp.float32),
             pltpu.VMEM((2, stride + 4, 8, ring), jnp.float32),
             pltpu.VMEM((3, cols // LANES, rows, LANES), jnp.float32),
             pltpu.VMEM((3, 2, 8, ring), jnp.float32),

time: 13.9 us -> 13.6 us (0.978)
  Pallas kernels: 11.9 us -> 11.6 us
    pallas_call x1, Pallas kernels: 11.9 us -> 11.6 us  [body(): pl.pallas_call(partial(kernel, (rows, cols, n_rows, n_cols)), out_shape=j...]
where the time goes in v4:
time: 13.6 us; the launch traced here: 13.4 us
  Pallas kernels  11.6 us (85%)
  local copies, waits for them, and re-layouts  1.77 us (13%)
    pallas_call x1, Pallas kernels, body(): pl.pallas_call(partial(kernel, (rows, cols, n_rows, n_cols)), out_shape=j...  11.6 us
    unnamed x1, local copies, waits for them, and re-layouts  1.77 us

profile of v4, /device:TPU:0, one launch (start us, length us, event | category | flops | bytes accessed | tf_op | source)
XLA Modules:
  0.0 13.4 jit_solution(8559521132951561229)
XLA Ops:
  0.0 11.6 %shard_map.46 = f32[3,128,256]{2,1,0:T(8,128)} custom-call(f32[3,128,256]{2,1,0:T(8,128)} %water.1, f32[128,256]{1,0:T(8,128)} %bed.1, s32[1,4,16]{2,1,0:T(4,128)} %active_hbm.1, s32[4,16]{1,0:T(4,128)} %roughness_hbm.1), custom_call_target="tpu_custom_call" | custom-call | flops 39321600 | bytes 1048576 | tf_op jit(solution)/shard_map/pallas_call | solution.py:441
  11.6 1.8 %copy.6 = f32[3,128,256]{2,1,0:T(8,128)} copy(f32[3,128,256]{2,1,0:T(8,128)} %shard_map.46) | data formatting | bytes 786432
